TPU v7x, 128 devices: a whole 4x4x4 slice. The times are simulated.
128 devices in a mesh: row: 8 (over x_hi, y), col: 16 (over x_lo, z, core).
Axes of the slice: x: 4 (x_hi: 2, x_lo: 2; x = x_hi * 2 + x_lo), y: 4, z: 4, core: 2. Of those that a mesh axis runs over, the one named last changes fastest.
Arguments:
- grad_out: bfloat16 [1024, 16384], P('col', 'row'), may hold values from -6 to 6
- gate: bfloat16 [1024, 26624], P('row', 'col'), may hold values from -8 to 8
- up: bfloat16 [1024, 26624], P('row', 'col'), may hold values from -6 to 6
- w_down: bfloat16 [16384, 26624], P('row', 'col'), may hold values from -0.046875 to 0.046875
Outputs:
- grad_gate: bfloat16 [1024, 26624], P('row', 'col')
- grad_up: bfloat16 [1024, 26624], P('row', 'col')
- grad_weight: bfloat16 [16384, 26624], P('row', 'col')
All inputs are finite; a program needn't handle non-finite values.
Results may differ from a plain program's by a relative error of at most 0.0049.
Values may be sent and summed in bfloat16 or wider, within the bound.
A program may use at most 128 MiB of HBM per device.

v0:
```python
import jax
import jax.numpy as jnp
from jax import lax
from jax.sharding import PartitionSpec as P


def swiglu_grads(grad_hidden, gate, up):
    gate_f = gate.astype(jnp.float32)
    up_f = up.astype(jnp.float32)
    sig = jax.nn.sigmoid(gate_f)
    silu = gate_f * sig
    hidden = (silu * up_f).astype(jnp.bfloat16)
    grad_up = (grad_hidden * silu).astype(jnp.bfloat16)
    grad_gate = (grad_hidden * up_f * sig * (1.0 + gate_f * (1.0 - sig))).astype(jnp.bfloat16)
    return (hidden, grad_gate, grad_up)


def outer_rows(left, right):
    return lax.dot_general(
        left, right, (((0,), (0,)), ((), ())), preferred_element_type=jnp.float32
    )


def on_device(grad_out, gate, up, w_down):
    gathered = lax.all_gather(grad_out, "col", axis=0, tiled=True)
    block = gathered
    grad_hidden = lax.psum_scatter(
        jnp.dot(block, w_down, preferred_element_type=jnp.float32),
        "row",
        scatter_dimension=0,
        tiled=True,
    )
    hidden, grad_gate, grad_up = swiglu_grads(grad_hidden, gate, up)
    block = gathered
    grad_weight = outer_rows(block, lax.all_gather(hidden, "row", axis=0, tiled=True))
    return (grad_gate, grad_up, grad_weight.astype(jnp.bfloat16))


def solution(mesh):
    in_specs = (P("col", "row"), P("row", "col"), P("row", "col"), P("row", "col"))
    out_specs = (P("row", "col"), P("row", "col"), P("row", "col"))
    return jax.shard_map(
        on_device, mesh=mesh, in_specs=in_specs, out_specs=out_specs, check_vma=False
    )
```

profile of v0, /device:TPU:0, one launch (start us, length us, event | category | flops | bytes accessed | tf_op | source)
XLA Modules:
  0.0 260.1 jit_solution(894505313614832688)
XLA Ops:
  7.2 0.0 all-gather.3.cloned.1.call-start
  7.2 0.7 all-gather.3.cloned.1.call-update
  7.9 0.0 reduce-scatter.2.cloned.1.call-start
  7.9 41.7 %all-gather.3.cloned.1.call-done = bf16[1024,2048]{1,0:T(8,128)(2,1)} async-done(((bf16[64,2048]{1,0:T(8,128)(2,1)}), bf16[1024,2048]{1,0:T(8,128)(2,1)}) %all-gather.3.cloned.1.call-update) | async-done | bytes 4194320 | tf_op jit(solution)/shard_map/all_gather | solution.py:25
  49.6 13.2 %fusion.9 = f32[1024,1664]{1,0:T(8,128)} fusion(bf16[1024,2048]{1,0:T(8,128)(2,1)} %all-gather.3.cloned.1.call-done, bf16[2048,1664]{1,0:T(8,128)(2,1)} %param.7), kind=kOutput, calls=%fused_computation.16 | convolution fusion | flops 6979321856 | bytes 17825792 | tf_op jit(solution)/shard_map/dot_general | solution.py:28
  62.9 0.0 copy-start
  62.9 0.0 copy-start.1
  62.9 0.0 reduce-scatter.2.cloned.1.call-update
  62.9 0.0 all-gather.5.cloned.1.call-start
  62.9 103.3 %reduce-scatter.2.cloned.1.call-done = f32[128,1664]{1,0:T(8,128)} async-done(((f32[1024,1664]{1,0:T(8,128)}), f32[128,1664]{1,0:T(8,128)}) %reduce-scatter.2.cloned.1.call-update) | async-done | bytes 851984 | tf_op jit(solution)/shard_map/reduce_scatter | solution.py:27
  166.2 0.0 copy-done
  166.2 0.0 copy-done.1
  166.2 2.6 multiply_convert_fusion
  168.8 0.0 all-gather.5.cloned.1.call-update
  168.8 63.2 %all-gather.5.cloned.1.call-done = bf16[1024,1664]{1,0:T(8,128)(2,1)} async-done(((bf16[128,1664]{1,0:T(8,128)(2,1)}), bf16[1024,1664]{1,0:T(8,128)(2,1)}) %all-gather.5.cloned.1.call-update) | async-done | bytes 3407888 | tf_op jit(solution)/shard_map/all_gather | solution.py:35
  232.1 11.9 %fusion = bf16[2048,1664]{0,1:T(8,128)(2,1)} fusion(bf16[1024,1664]{1,0:T(8,128)(2,1)} %all-gather.5.cloned.1.call-done, bf16[1024,2048]{1,0:T(8,128)(2,1)} %all-gather.3.cloned.1.call-done), kind=kOutput, calls=%fused_computation.1 | convolution fusion | flops 6982729728 | bytes 14417920 | tf_op jit(solution)/shard_map/dot_general | solution.py:19
  243.9 9.7 %copy.7 = bf16[2048,1664]{1,0:T(8,128)(2,1)} copy(bf16[2048,1664]{0,1:T(8,128)(2,1)} %fusion) | data formatting | bytes 13631488
Async XLA Ops:
  7.2 42.5 %all-gather.3.cloned.1.call-start = ((), (), s32[]{:S(2)}) async-start(), calls=%async_computation.1 | async-start | bytes 4456448 | tf_op jit(solution)/shard_map/all_gather | solution.py:25
  7.9 158.3 %reduce-scatter.2.cloned.1.call-start = ((), (), s32[]{:S(2)}) async-start(), calls=%async_computation.2 | async-start | bytes 7667712 | tf_op jit(solution)/shard_map/reduce_scatter | solution.py:27
  62.9 103.3 %copy-start = (bf16[128,1664]{1,0:T(8,128)(2,1)S(1)}, bf16[128,1664]{1,0:T(8,128)(2,1)}, u32[]{:S(2)}) copy-start(bf16[128,1664]{1,0:T(8,128)(2,1)} %param.5) | copy-start | bytes 1277956
  62.9 103.3 %copy-start.1 = (bf16[128,1664]{1,0:T(8,128)(2,1)S(1)}, bf16[128,1664]{1,0:T(8,128)(2,1)}, u32[]{:S(2)}) copy-start(bf16[128,1664]{1,0:T(8,128)(2,1)} %param.6) | copy-start | bytes 1277956
  62.9 169.2 %all-gather.5.cloned.1.call-start = ((), (), s32[]{:S(2)}) async-start(), calls=%async_computation.3 | async-start | bytes 3833856 | tf_op jit(solution)/shard_map/all_gather | solution.py:35
Sparse Core Ops, SparseCore 0:
  9.7 39.8 all-gather.2
  63.0 103.1 reduce-scatter.1
  169.1 62.9 all-gather.4
where the time goes:
time: 261 us; the launch traced here: 260 us
  waiting for transfers between devices  209 us (80%)
  matrix products  25.1 us (10%)
  between operations  13.7 us (5%)
  local copies, waits for them, and re-layouts  9.66 us (4%)
    reduce_scatter x1, waiting for transfers between devices, on_device(): lax.psum_scatter(jnp.dot(block, w_down, preferred_element_type=jnp.float3...  103 us
    all_gather x1, waiting for transfers between devices, on_device(): lax.all_gather(hidden, 'row', axis=0, tiled=True)  63.2 us
    all_gather x1, waiting for transfers between devices, on_device(): gathered = lax.all_gather(grad_out, 'col', axis=0, tiled=True)  41.7 us
    dot_general x1, matrix products, on_device(): jnp.dot(block, w_down, preferred_element_type=jnp.float32)  13.2 us
    dot_general x1, matrix products, outer_rows(): lax.dot_general(left, right, (((0,), (0,)), ((), ())), preferred_element_...  11.9 us
    unnamed x5, local copies, waits for them, and re-layouts  9.66 us
  transfers between devices with their start and end apart: 3, of which 3 were waited for; matrix products, arithmetic and copies ran while one was open for 0% of the time, Pallas kernels for 0%

commit v1 on v0

v1 whole, which is shorter than its diff:
```python
import functools

import jax
import jax.numpy as jnp
from jax import lax
from jax.experimental import pallas as pl
from jax.experimental.pallas import tpu as pltpu
from jax.sharding import PartitionSpec as P

MESH = pl.DeviceIdType.MESH
BF16, F32 = jnp.bfloat16, jnp.float32
NY, NX = 4, 2
COPIES = 96


def kernel(
    split, go_in, gate_in, up_in, w_in, gg_out, gu_out, gw_out,
    go, w, acc, hid, gate, up, silu, slope, gw, gg, gu,
    pfar, pnear, px, qx, qfar, qnear, local, ssem, rsem,
):
    tokens, units = hid.shape
    features = go.shape[1]
    own = tokens // (NX * NY)
    half, part = own // 2, own // 2
    group = NX * own
    row, col = lax.axis_index("row"), lax.axis_index("col")
    xh, y = row // NY, row % NY
    xl, z, c = col // (2 * NY), (col // 2) % NY, col % 2
    yp, ym, yf = (y + 1) % NY, (y + 3) % NY, (y + 2) % NY
    zp, zm, zf = (z + 1) % NY, (z + 3) % NY, (z + 2) % NY
    up_y, dn_y, over_x = (xh * NY + yp, col), (xh * NY + ym, col), ((1 - xh) * NY + y, col)

    def at_col(a, b, d):
        return (row, a * (2 * NY) + b * 2 + d)

    up_z, dn_z = at_col(xl, zp, c), at_col(xl, zm, c)
    next_x, other = at_col(1 - xl, z, c), at_col(xl, z, 1 - c)
    peers = (up_y, dn_y, over_x, up_z, dn_z, next_x, other)

    cols = (pl.ds(0, split), pl.ds(split, units - split))

    def rows(a, b, h=None):
        start = b * group + a * own
        if h is None:
            return pl.ds(pl.multiple_of(start, own), own)
        return pl.ds(pl.multiple_of(start + h * half, half), half)

    def panel(a, b, d, h=None):
        start = b * group + a * own + d * part
        if h is None:
            return pl.ds(pl.multiple_of(start, part), part)
        return pl.ds(pl.multiple_of(start + h * (part // 2), part // 2), part // 2)

    names, sent = {}, []

    def index(name):
        return names.setdefault(name, len(names))

    def send(name, src, dst, device):
        k = index(name)
        copy = pltpu.make_async_remote_copy(src, dst, ssem.at[k], rsem.at[k], device_id=device, device_id_type=MESH)
        copy.start()
        sent.append(copy)

    def arrived(name, dst):
        k = index(name)
        pltpu.make_async_remote_copy(dst, dst, ssem.at[k], rsem.at[k], device_id=other, device_id_type=MESH).wait_recv()

    loads = [
        pltpu.make_async_copy(gate_in, gate, local.at[0]),
        pltpu.make_async_copy(up_in, up, local.at[1]),
        pltpu.make_async_copy(go_in, go.at[panel(xl, z, c)], local.at[2]),
        pltpu.make_async_copy(w_in, w, local.at[3]),
    ]
    for load in loads:
        load.start()
    barrier = pltpu.get_barrier_semaphore()
    for peer in peers:
        pl.semaphore_signal(barrier, inc=1, device_id=peer, device_id_type=MESH)
    pl.semaphore_wait(barrier, len(peers))

    def gsend(name, a, b, d, device, h=None, src=None):
        ref = go.at[panel(a, b, d, h)]
        send(name, ref if src is None else src, ref, device)

    def garrived(name, a, b, d, h=None):
        arrived(name, go.at[panel(a, b, d, h)])

    gsend("g_next", xl, z, c, next_x, src=go_in)
    gsend("g_up", xl, z, c, up_z, src=go_in)
    gsend("g_dn", xl, z, c, dn_z, src=go_in)
    gsend("g_other", xl, z, c, other, src=go_in)

    def hsend(name, a, b, p, device, h):
        ref = hid.at[rows(a, b, h), cols[p]]
        send((name, p, h), ref, ref, device)

    def harrived(name, a, b, p, h):
        arrived((name, p, h), hid.at[rows(a, b, h), cols[p]])

    def activate(p, h):
        step = 16

        @pl.loop(0, half // step)
        def _(i):
            at = pl.ds(pl.multiple_of(h * half + i * step, step), step)
            to = pl.ds(pl.multiple_of(y * group + xh * own + h * half + i * step, step), step)
            v, u = gate[at, cols[p]].astype(F32), up[at, cols[p]].astype(F32)
            s = jax.nn.sigmoid(v)
            act = v * s
            silu[at, cols[p]] = act
            slope[at, cols[p]] = u * s * (1.0 + v * (1.0 - s))
            hid[to, cols[p]] = (act * u).astype(BF16)

    loads[0].wait()
    loads[1].wait()
    for p in (1, 0):
        activate(p, 0)
        hsend("h_up", xh, y, p, up_y, 0)
        activate(p, 1)
        hsend("h_dn", xh, y, p, dn_y, 1)
        hsend("h_up", xh, y, p, up_y, 1)
        hsend("h_dn", xh, y, p, dn_y, 0)
        if p == 0:
            for q in (0, 1):
                for h in (0, 1):
                    hsend("h_x", xh, y, q, over_x, h)

    def near_h(p):
        harrived("h_up", xh, ym, p, 0)
        hsend("h_up2", xh, ym, p, up_y, 0)
        harrived("h_dn", xh, yp, p, 1)
        hsend("h_dn2", xh, yp, p, dn_y, 1)
        harrived("h_up", xh, ym, p, 1)
        harrived("h_dn", xh, yp, p, 0)
        if p == 1:
            for h in (0, 1):
                hsend("h_xm", xh, ym, p, over_x, h)
                hsend("h_xp", xh, yp, p, over_x, h)

    def project(b):
        at = pl.ds(pl.multiple_of(b * group, group), group)
        wide = 256

        @pl.loop(0, units // wide)
        def _(j):
            to = pl.ds(pl.multiple_of(j * wide, wide), wide)
            acc[at, to] = jnp.dot(go[at, :], w[:, to], preferred_element_type=F32).astype(BF16)

        rest = units % wide
        if rest:
            to = pl.ds(units - rest, rest)
            acc[at, to] = jnp.dot(go[at, :], w[:, to], preferred_element_type=F32).astype(BF16)

    near_h(1)
    garrived("g_next", 1 - xl, z, c)
    gsend("g_xup", 1 - xl, z, c, up_z)
    gsend("g_xdn", 1 - xl, z, c, dn_z)
    gsend("g_xother", 1 - xl, z, c, other)
    garrived("g_up", xl, zm, c)
    gsend("g_up2", xl, zm, c, up_z, 0)
    gsend("g_upo", xl, zm, c, other)
    garrived("g_dn", xl, zp, c)
    gsend("g_dn2", xl, zp, c, dn_z, 1)
    gsend("g_dno", xl, zp, c, other)
    loads[2].wait()
    loads[3].wait()
    garrived("g_other", xl, z, 1 - c)
    garrived("g_xother", 1 - xl, z, 1 - c)
    project(z)
    near_h(0)
    for h in (0, 1):
        harrived("h_x", 1 - xh, y, 0, h)
    hsend("h_gup", 1 - xh, y, 0, up_y, 0)
    hsend("h_gdn", 1 - xh, y, 0, dn_y, 1)
    hsend("h_gup", 1 - xh, y, 0, up_y, 1)
    hsend("h_gdn", 1 - xh, y, 0, dn_y, 0)
    garrived("g_xup", 1 - xl, zm, c)
    gsend("g_xup2", 1 - xl, zm, c, up_z, 0)
    gsend("g_xupo", 1 - xl, zm, c, other)
    garrived("g_xdn", 1 - xl, zp, c)
    gsend("g_xdn2", 1 - xl, zp, c, dn_z, 1)
    gsend("g_xdno", 1 - xl, zp, c, other)
    harrived("h_up2", xh, yf, 1, 0)
    hsend("h_xf", xh, yf, 1, over_x, 0)
    harrived("h_dn2", xh, yf, 1, 1)
    hsend("h_xf", xh, yf, 1, over_x, 1)
    garrived("g_upo", xl, zm, 1 - c)
    garrived("g_xupo", 1 - xl, zm, 1 - c)
    project(zm)
    garrived("g_up2", xl, zf, c, 0)
    garrived("g_dn2", xl, zf, c, 1)
    gsend("g_faro", xl, zf, c, other)
    garrived("g_dno", xl, zp, 1 - c)
    garrived("g_xdno", 1 - xl, zp, 1 - c)
    project(zp)
    garrived("g_xup2", 1 - xl, zf, c, 0)
    garrived("g_xdn2", 1 - xl, zf, c, 1)
    gsend("g_xfaro", 1 - xl, zf, c, other)
    harrived("h_gup", 1 - xh, ym, 0, 0)
    hsend("h_gup2", 1 - xh, ym, 0, up_y, 0)
    harrived("h_gdn", 1 - xh, yp, 0, 1)
    hsend("h_gdn2", 1 - xh, yp, 0, dn_y, 1)
    garrived("g_faro", xl, zf, 1 - c)
    garrived("g_xfaro", 1 - xl, zf, 1 - c)
    project(zf)

    sides = (1 - xh, xh)
    order = (yf, yp, ym, y)
    for i, b in enumerate(order):
        send(("q_x", i), acc.at[rows(1 - xh, b), cols[1]], qx.at[i], over_x)
    for s in (0, 1):
        send(("p_far_up", s), acc.at[rows(sides[s], yf, 0), cols[0]], pfar.at[s, 0], up_y)
        send(("p_far_dn", s), acc.at[rows(sides[s], yf, 1), cols[0]], pfar.at[s, 1], dn_y)

    def pnear_to(d, s, h):
        name, b, device = (("p_up", yp, up_y), ("p_dn", ym, dn_y))[d]
        send((name, s, h), acc.at[rows(sides[s], b, h), cols[0]], pnear.at[s, d, pl.ds(h * half, half)], device)

    for s in (0, 1):
        pnear_to(0, s, 1)
        pnear_to(1, s, 0)

    def add(at, p, ref):
        acc[at, cols[p]] = (acc[at, cols[p]].astype(F32) + ref[...].astype(F32)).astype(BF16)

    def meet(s):
        for d, (name, b) in enumerate((("p_far_up", yp), ("p_far_dn", ym))):
            arrived((name, s), pfar.at[s, d])
            add(rows(sides[s], b, d), 0, pfar.at[s, d])
            pnear_to(d, s, d)

    stores = []

    def outer(f):
        deep = features // 4
        at = pl.ds(f * deep, deep)
        for start, wide in ((0, 512), (512, 512), (1024, 640)):
            to = pl.ds(start, wide)
            gw[at, to] = lax.dot_general(
                go[:, at], hid[:, to], (((0,), (0,)), ((), ())), preferred_element_type=F32
            ).astype(BF16)
        store = pltpu.make_async_copy(gw.at[at], gw_out.at[at], local.at[4 + f])
        store.start()
        stores.append(store)

    for p in (0, 1):
        for h in (0, 1):
            if p == 1:
                harrived("h_x", 1 - xh, y, 1, h)
                harrived("h_xm", 1 - xh, ym, 1, h)
                harrived("h_xp", 1 - xh, yp, 1, h)
                harrived("h_xf", 1 - xh, yf, 1, h)
    harrived("h_up2", xh, yf, 0, 0)
    harrived("h_dn2", xh, yf, 0, 1)
    harrived("h_gup", 1 - xh, ym, 0, 1)
    harrived("h_gdn", 1 - xh, yp, 0, 0)
    harrived("h_gup2", 1 - xh, yf, 0, 0)
    harrived("h_gdn2", 1 - xh, yf, 0, 1)
    outer(0)
    meet(0)
    outer(1)
    meet(1)
    outer(2)

    def qadd(i):
        arrived(("q_x", i), qx.at[i])
        add(rows(xh, order[i]), 1, qx.at[i])

    def qnear_to(d, h):
        name, b, device = (("q_up", yp, up_y), ("q_dn", ym, dn_y))[d]
        send((name, h), acc.at[rows(xh, b, h), cols[1]], qnear.at[d, pl.ds(h * half, half)], device)

    qadd(0)
    send("q_far_up", acc.at[rows(xh, yf, 0), cols[1]], qfar.at[0], up_y)
    send("q_far_dn", acc.at[rows(xh, yf, 1), cols[1]], qfar.at[1], dn_y)
    outer(3)
    qadd(1)
    qnear_to(0, 1)
    qadd(2)
    qnear_to(1, 0)
    for d, (name, b) in enumerate((("q_far_up", yp), ("q_far_dn", ym))):
        arrived(name, qfar.at[d])
        add(rows(xh, b, d), 1, qfar.at[d])
        qnear_to(d, d)

    def near_sum(s):
        for h in (0, 1):
            arrived(("p_up", s, h), pnear.at[s, 0, pl.ds(h * half, half)])
            arrived(("p_dn", s, h), pnear.at[s, 1, pl.ds(h * half, half)])

    near_sum(0)
    for h in (0, 1):
        at, piece = rows(1 - xh, y, h), pl.ds(h * half, half)
        total = acc[at, cols[0]].astype(F32) + pnear[0, 0, piece].astype(F32) + pnear[0, 1, piece].astype(F32)
        acc[at, cols[0]] = total.astype(BF16)
        send(("p_x", h), acc.at[at, cols[0]], px.at[piece], over_x)
    qadd(3)

    def finish(p, piece, total):
        gu[piece, cols[p]] = (total * silu[piece, cols[p]]).astype(BF16)
        gg[piece, cols[p]] = (total * slope[piece, cols[p]]).astype(BF16)

    near_sum(1)
    for h in (0, 1):
        piece = pl.ds(h * half, half)
        arrived(("p_x", h), px.at[piece])
        total = acc[rows(xh, y, h), cols[0]].astype(F32) + px[piece].astype(F32)
        total = total + pnear[1, 0, piece].astype(F32) + pnear[1, 1, piece].astype(F32)
        finish(0, piece, total)
    for h in (0, 1):
        piece = pl.ds(h * half, half)
        arrived(("q_up", h), qnear.at[0, piece])
        arrived(("q_dn", h), qnear.at[1, piece])
        total = acc[rows(xh, y, h), cols[1]].astype(F32)
        total = total + qnear[0, piece].astype(F32) + qnear[1, piece].astype(F32)
        finish(1, piece, total)
    stores.append(pltpu.make_async_copy(gg, gg_out, local.at[8]))
    stores.append(pltpu.make_async_copy(gu, gu_out, local.at[9]))
    stores[-1].start()
    stores[-2].start()
    for copy in sent:
        copy.wait_send()
    for store in stores:
        store.wait()


def on_device(grad_out, gate, up, w_down):
    own, units = gate.shape
    features = w_down.shape[0]
    tokens = own * NX * NY
    split = 1024
    rest = units - split
    half = own // 2
    anywhere = pl.BlockSpec(memory_space=pl.ANY)
    return pl.pallas_call(
        functools.partial(kernel, split),
        out_shape=(
            jax.ShapeDtypeStruct((own, units), BF16),
            jax.ShapeDtypeStruct((own, units), BF16),
            jax.ShapeDtypeStruct((features, units), BF16),
        ),
        in_specs=[anywhere] * 4,
        out_specs=(anywhere,) * 3,
        scratch_shapes=[
            pltpu.VMEM((tokens, features), BF16),
            pltpu.VMEM((features, units), BF16),
            pltpu.VMEM((tokens, units), BF16),
            pltpu.VMEM((tokens, units), BF16),
            pltpu.VMEM((own, units), BF16),
            pltpu.VMEM((own, units), BF16),
            pltpu.VMEM((own, units), F32),
            pltpu.VMEM((own, units), F32),
            pltpu.VMEM((features, units), BF16),
            pltpu.VMEM((own, units), BF16),
            pltpu.VMEM((own, units), BF16),
            pltpu.VMEM((2, 2, half, split), BF16),
            pltpu.VMEM((2, 2, own, split), BF16),
            pltpu.VMEM((own, split), BF16),
            pltpu.VMEM((NY, own, rest), BF16),
            pltpu.VMEM((2, half, rest), BF16),
            pltpu.VMEM((2, own, rest), BF16),
            pltpu.SemaphoreType.DMA((10,)),
            pltpu.SemaphoreType.DMA((COPIES,)),
            pltpu.SemaphoreType.DMA((COPIES,)),
        ],
        compiler_params=pltpu.CompilerParams(
            collective_id=0, has_side_effects=True, vmem_limit_bytes=56 * 2**20
        ),
        cost_estimate=pl.CostEstimate(
            flops=4 * tokens * features * units, bytes_accessed=4 * features * units, transcendentals=own * units
        ),
    )(grad_out, gate, up, w_down)


def solution(mesh):
    return jax.shard_map(
        on_device,
        mesh=mesh,
        in_specs=(P("col", "row"), P("row", "col"), P("row", "col"), P("row", "col")),
        out_specs=(P("row", "col"),) * 3,
        check_vma=False,
    )
```

time: 261 us -> 76.4 us (0.29)
  waiting for transfers between devices: 209 us -> 0 us
  Pallas kernels: 0 us -> 65.6 us
  matrix products: 25.1 us -> 0 us
  between operations: 13.7 us -> 0.64 us
    all_gather x2 -> x0, waiting for transfers between devices: 105 us -> none  [the longest x1 63.2 us: on_device(): lax.all_gather(hidden, 'row', axis=0, tiled=True)]
    reduce_scatter x1 -> x0, waiting for transfers between devices: 103 us -> none  [on_device(): lax.psum_scatter(jnp.dot(block, w_down, preferred_element_type=jnp.float3...]
    pallas_call x0 -> x1, Pallas kernels: none -> 65.6 us  [on_device(): pl.pallas_call(functools.partial(kernel, split), out_shape=(jax.ShapeDtyp...]
    dot_general x2 -> x0, matrix products: 25.1 us -> none  [the longest x1 13.2 us: on_device(): jnp.dot(block, w_down, preferred_element_type=jnp.float32)]
    unnamed x5 -> x3, local copies, waits for them, and re-layouts: 9.66 us -> 9.89 us
  transfers between devices with their start and end apart: 3 -> 0, of which waited for: 3 -> 0; matrix products, arithmetic and copies ran while one was open for 0% -> 0% of each run, Pallas kernels for 0% -> 0%
where the time goes in v1:
time: 76.4 us; the launch traced here: 76.2 us
  Pallas kernels  65.6 us (86%)
  local copies, waits for them, and re-layouts  9.89 us (13%)
    pallas_call x1, Pallas kernels, on_device(): pl.pallas_call(functools.partial(kernel, split), out_shape=(jax.ShapeDtyp...  65.6 us
    unnamed x3, local copies, waits for them, and re-layouts  9.89 us

profile of v1, /device:TPU:0, one launch (start us, length us, event | category | flops | bytes accessed | tf_op | source)
XLA Modules:
  0.0 76.2 jit_solution(13001229556278621223)
XLA Ops:
  0.6 65.6 %shard_map.67 = (bf16[128,1664]{1,0:T(8,128)(2,1)}, bf16[128,1664]{1,0:T(8,128)(2,1)}, bf16[2048,1664]{1,0:T(8,128)(2,1)}) custom-call(bf16[64,2048]{1,0:T(8,128)(2,1)} %go_in.1, bf16[128,1664]{1,0:T(8,128)(2,1)} %gate_in.1, bf16[128,1664]{1,0:T(8,128)(2,1)} %up_in.1, bf16[2048,1664]{1,0:T(8,128)(2,1)} %w_in.1), custom_call_target="tpu_custom_call" | custom-call | flops 13958643712 | bytes 13631488 | tf_op jit(solution)/shard_map/pallas_call | solution.py:336
  66.3 1.8 %copy.10 = bf16[128,1664]{1,0:T(8,128)(2,1)} copy(bf16[128,1664]{1,0:T(8,128)(2,1)} %get-tuple-element.6) | data formatting | bytes 851968
  68.1 1.8 %copy.11 = bf16[128,1664]{1,0:T(8,128)(2,1)} copy(bf16[128,1664]{1,0:T(8,128)(2,1)} %get-tuple-element.7) | data formatting | bytes 851968
  69.9 6.3 %copy.12 = bf16[2048,1664]{1,0:T(8,128)(2,1)} copy(bf16[2048,1664]{1,0:T(8,128)(2,1)} %get-tuple-element.8) | data formatting | bytes 13631488

commit v2 on v1

v2 whole, which is shorter than its diff:
```python
import functools

import jax
import jax.numpy as jnp
from jax import lax
from jax.experimental import pallas as pl
from jax.experimental.pallas import tpu as pltpu
from jax.sharding import PartitionSpec as P

MESH = pl.DeviceIdType.MESH
BF16, F32 = jnp.bfloat16, jnp.float32
NY, NX = 4, 2
COPIES = 96


def kernel(
    hsplit, rsplit, go_in, gate_in, up_in, w_in, gg_out, gu_out, gw_out,
    go, w, acc, hid, gate, up, silu, slope, gw, gg, gu,
    pfar, pnear, px, qx, qfar, qnear, local, ssem, rsem,
):
    tokens, units = hid.shape
    features = go.shape[1]
    own = tokens // (NX * NY)
    half, part = own // 2, own // 2
    group = NX * own
    row, col = lax.axis_index("row"), lax.axis_index("col")
    xh, y = row // NY, row % NY
    xl, z, c = col // (2 * NY), (col // 2) % NY, col % 2
    yp, ym, yf = (y + 1) % NY, (y + 3) % NY, (y + 2) % NY
    zp, zm, zf = (z + 1) % NY, (z + 3) % NY, (z + 2) % NY
    up_y, dn_y, over_x = (xh * NY + yp, col), (xh * NY + ym, col), ((1 - xh) * NY + y, col)

    def at_col(a, b, d):
        return (row, a * (2 * NY) + b * 2 + d)

    up_z, dn_z = at_col(xl, zp, c), at_col(xl, zm, c)
    next_x, other = at_col(1 - xl, z, c), at_col(xl, z, 1 - c)
    peers = (up_y, dn_y, over_x, up_z, dn_z, next_x, other)

    hcols = (pl.ds(0, hsplit), pl.ds(hsplit, units - hsplit))
    rcols = (pl.ds(0, rsplit), pl.ds(rsplit, units - rsplit))

    def rows(a, b, h=None):
        start = b * group + a * own
        if h is None:
            return pl.ds(pl.multiple_of(start, own), own)
        return pl.ds(pl.multiple_of(start + h * half, half), half)

    def panel(a, b, d, h=None):
        start = b * group + a * own + d * part
        if h is None:
            return pl.ds(pl.multiple_of(start, part), part)
        return pl.ds(pl.multiple_of(start + h * (part // 2), part // 2), part // 2)

    names, sent = {}, {}

    def index(name):
        return names.setdefault(name, len(names))

    def send(name, src, dst, device, note=True):
        k = index(name)
        if note:
            sent[name] = dst
        pltpu.make_async_remote_copy(src, dst, ssem.at[k], rsem.at[k], device_id=device, device_id_type=MESH).start()

    def drain():
        for name, ref in sent.items():
            k = index(name)
            pltpu.make_async_remote_copy(ref, ref, ssem.at[k], rsem.at[k], device_id=other, device_id_type=MESH).wait_send()
        sent.clear()

    def arrived(name, dst):
        k = index(name)
        pltpu.make_async_remote_copy(dst, dst, ssem.at[k], rsem.at[k], device_id=other, device_id_type=MESH).wait_recv()

    loads = [
        pltpu.make_async_copy(gate_in, gate, local.at[0]),
        pltpu.make_async_copy(up_in, up, local.at[1]),
        pltpu.make_async_copy(go_in, go.at[panel(xl, z, c)], local.at[2]),
        pltpu.make_async_copy(w_in, w, local.at[3]),
    ]
    barrier = pltpu.get_barrier_semaphore()
    for peer in peers:
        pl.semaphore_signal(barrier, inc=1, device_id=peer, device_id_type=MESH)
    for load in loads[:3]:
        load.start()

    def gsend(name, a, b, d, device, h=None, src=None):
        ref = go.at[panel(a, b, d, h)]
        send((name, h), ref if src is None else src, ref, device)

    def garrived(name, a, b, d, h=None):
        arrived((name, h), go.at[panel(a, b, d, h)])

    def hsend(name, a, b, p, device, h):
        ref = hid.at[rows(a, b, h), hcols[p]]
        send((name, p, h), ref, ref, device)

    def harrived(name, a, b, p, h):
        arrived((name, p, h), hid.at[rows(a, b, h), hcols[p]])

    def activate(p, h):
        step = 16

        @pl.loop(0, half // step)
        def _(i):
            at = pl.ds(pl.multiple_of(h * half + i * step, step), step)
            to = pl.ds(pl.multiple_of(y * group + xh * own + h * half + i * step, step), step)
            v, u = gate[at, hcols[p]].astype(F32), up[at, hcols[p]].astype(F32)
            s = jax.nn.sigmoid(v)
            act = v * s
            silu[at, hcols[p]] = act
            slope[at, hcols[p]] = u * s * (1.0 + v * (1.0 - s))
            hid[to, hcols[p]] = (act * u).astype(BF16)

    loads[0].wait()
    loads[1].wait()
    loads[3].start()
    for p in (0, 1):
        for h in (0, 1):
            activate(p, h)
    pl.semaphore_wait(barrier, len(peers))
    pieces = [go_in.at[pl.ds(h * (part // 2), part // 2)] for h in (0, 1)]
    for h in (0, 1):
        gsend("g_next", xl, z, c, next_x, h, pieces[h])
        gsend("g_up", xl, z, c, up_z, h, pieces[h])
        gsend("g_dn", xl, z, c, dn_z, 1 - h, pieces[1 - h])
        hsend("h_up", xh, y, 0, up_y, h)
        hsend("h_dn", xh, y, 0, dn_y, 1 - h)
        hsend("h_x", xh, y, 0, over_x, h)
    for h in (0, 1):
        hsend("h_up", xh, y, 1, up_y, h)
        hsend("h_dn", xh, y, 1, dn_y, 1 - h)
        hsend("h_x", xh, y, 1, over_x, h)
    gsend("g_other", xl, z, c, other, src=go_in)

    def project(b):
        at = pl.ds(pl.multiple_of(b * group, group), group)
        wide = 256

        @pl.loop(0, units // wide)
        def _(j):
            to = pl.ds(pl.multiple_of(j * wide, wide), wide)
            acc[at, to] = jnp.dot(go[at, :], w[:, to], preferred_element_type=F32).astype(BF16)

        rest = units % wide
        if rest:
            to = pl.ds(units - rest, rest)
            acc[at, to] = jnp.dot(go[at, :], w[:, to], preferred_element_type=F32).astype(BF16)

    sides = (1 - xh, xh)
    order = (z, zm, zp, zf)

    def pfar_to(s, d):
        name, device = (("p_far_up", up_y), ("p_far_dn", dn_y))[d]
        send((name, s), acc.at[rows(sides[s], yf, d), rcols[0]], pfar.at[s, d], device, False)

    def pnear_to(s, d, h):
        name, b, device = (("p_up", yp, up_y), ("p_dn", ym, dn_y))[d]
        to = pnear.at[s, d, pl.ds(h * half, half)]
        send((name, s, h), acc.at[rows(sides[s], b, h), rcols[0]], to, device, False)

    def release(i):
        send(("q_x", i), acc.at[rows(1 - xh, order[i]), rcols[1]], qx.at[i], over_x)
        away = (order[i] - y + NY) % NY

        @pl.when(away == 2)
        def _():
            for s in (0, 1):
                pfar_to(s, 0)
                pfar_to(s, 1)

        @pl.when(away == 1)
        def _():
            for s in (0, 1):
                pnear_to(s, 0, 1)

        @pl.when(away == 3)
        def _():
            for s in (0, 1):
                pnear_to(s, 1, 0)

    for h in (0, 1):
        garrived("g_next", 1 - xl, z, c, h)
        gsend("g_xup", 1 - xl, z, c, up_z, h)
        gsend("g_xdn", 1 - xl, z, c, dn_z, h)
        gsend("g_xother", 1 - xl, z, c, other, h)
        if h == 0:
            harrived("h_up", xh, ym, 0, 0)
            hsend("h_up2", xh, ym, 0, up_y, 0)
            harrived("h_dn", xh, yp, 0, 1)
            hsend("h_dn2", xh, yp, 0, dn_y, 1)
    garrived("g_up", xl, zm, c, 0)
    gsend("g_up2", xl, zm, c, up_z, 0)
    garrived("g_dn", xl, zp, c, 1)
    gsend("g_dn2", xl, zp, c, dn_z, 1)
    garrived("g_up", xl, zm, c, 1)
    gsend("g_upo", xl, zm, c, other)
    garrived("g_dn", xl, zp, c, 0)
    gsend("g_dno", xl, zp, c, other)
    harrived("h_x", 1 - xh, y, 0, 0)
    hsend("h_gup", 1 - xh, y, 0, up_y, 0)
    hsend("h_gdn", 1 - xh, y, 0, dn_y, 0)
    harrived("h_up", xh, ym, 1, 0)
    hsend("h_up2", xh, ym, 1, up_y, 0)
    hsend("h_xm", xh, ym, 1, over_x, 0)
    harrived("h_dn", xh, yp, 1, 1)
    hsend("h_dn2", xh, yp, 1, dn_y, 1)
    hsend("h_xp", xh, yp, 1, over_x, 1)
    harrived("h_x", 1 - xh, y, 0, 1)
    hsend("h_gdn", 1 - xh, y, 0, dn_y, 1)
    hsend("h_gup", 1 - xh, y, 0, up_y, 1)
    harrived("h_up", xh, ym, 1, 1)
    hsend("h_xm", xh, ym, 1, over_x, 1)
    harrived("h_dn", xh, yp, 1, 0)
    hsend("h_xp", xh, yp, 1, over_x, 0)
    loads[2].wait()
    loads[3].wait()
    garrived("g_other", xl, z, 1 - c)
    garrived("g_xother", 1 - xl, z, 1 - c, 0)
    garrived("g_xother", 1 - xl, z, 1 - c, 1)
    project(z)
    garrived("g_xup", 1 - xl, zm, c, 0)
    gsend("g_xup2", 1 - xl, zm, c, up_z, 0)
    garrived("g_xdn", 1 - xl, zp, c, 1)
    gsend("g_xdn2", 1 - xl, zp, c, dn_z, 1)
    garrived("g_xup", 1 - xl, zm, c, 1)
    gsend("g_xupo", 1 - xl, zm, c, other)
    garrived("g_xdn", 1 - xl, zp, c, 0)
    gsend("g_xdno", 1 - xl, zp, c, other)
    garrived("g_upo", xl, zm, 1 - c)
    garrived("g_xupo", 1 - xl, zm, 1 - c)
    project(zm)
    harrived("h_gup", 1 - xh, ym, 0, 0)
    hsend("h_gup2", 1 - xh, ym, 0, up_y, 0)
    harrived("h_up2", xh, yf, 1, 0)
    hsend("h_xf", xh, yf, 1, over_x, 0)
    harrived("h_dn2", xh, yf, 1, 1)
    hsend("h_xf", xh, yf, 1, over_x, 1)
    harrived("h_gdn", 1 - xh, yp, 0, 1)
    hsend("h_gdn2", 1 - xh, yp, 0, dn_y, 1)
    release(0)
    release(1)
    garrived("g_up2", xl, zf, c, 0)
    garrived("g_dn2", xl, zf, c, 1)
    gsend("g_faro", xl, zf, c, other)
    garrived("g_dno", xl, zp, 1 - c)
    garrived("g_xdno", 1 - xl, zp, 1 - c)
    project(zp)
    release(2)
    garrived("g_xup2", 1 - xl, zf, c, 0)
    garrived("g_xdn2", 1 - xl, zf, c, 1)
    gsend("g_xfaro", 1 - xl, zf, c, other)
    garrived("g_faro", xl, zf, 1 - c)
    garrived("g_xfaro", 1 - xl, zf, 1 - c)
    project(zf)
    release(3)

    def add(at, p, ref):
        acc[at, rcols[p]] = (acc[at, rcols[p]].astype(F32) + ref[...].astype(F32)).astype(BF16)

    def meet(s):
        for d, (name, b) in enumerate((("p_far_up", yp), ("p_far_dn", ym))):
            arrived((name, s), pfar.at[s, d])
            add(rows(sides[s], b, d), 0, pfar.at[s, d])
            pnear_to(s, d, d)

    stores = []
    deep = features // 8

    def outer(f):
        at = pl.ds(f * deep, deep)
        gw[at, :] = lax.dot_general(
            go[:, at], hid[...], (((0,), (0,)), ((), ())), preferred_element_type=F32
        ).astype(BF16)
        store = pltpu.make_async_copy(gw.at[at], gw_out.at[at], local.at[4 + f])
        store.start()
        stores.append(store)

    def qadd(i):
        arrived(("q_x", i), qx.at[i])
        add(rows(xh, order[i]), 1, qx.at[i])

    def qfar_to(d):
        name, device = (("q_far_up", up_y), ("q_far_dn", dn_y))[d]
        send((name, 0), acc.at[rows(xh, yf, d), rcols[1]], qfar.at[d], device)

    def qnear_to(d, h):
        name, b, device = (("q_up", yp, up_y), ("q_dn", ym, dn_y))[d]
        send((name, h), acc.at[rows(xh, b, h), rcols[1]], qnear.at[d, pl.ds(h * half, half)], device)

    for h in (0, 1):
        harrived("h_x", 1 - xh, y, 1, h)
        harrived("h_xm", 1 - xh, ym, 1, h)
        harrived("h_xp", 1 - xh, yp, 1, h)
        harrived("h_xf", 1 - xh, yf, 1, h)
    harrived("h_up", xh, ym, 0, 1)
    harrived("h_dn", xh, yp, 0, 0)
    harrived("h_up2", xh, yf, 0, 0)
    harrived("h_dn2", xh, yf, 0, 1)
    harrived("h_gup", 1 - xh, ym, 0, 1)
    harrived("h_gdn", 1 - xh, yp, 0, 0)
    harrived("h_gup2", 1 - xh, yf, 0, 0)
    harrived("h_gdn2", 1 - xh, yf, 0, 1)
    for f in range(4):
        outer(f)
    qadd(0)
    outer(4)
    qadd(1)
    meet(0)
    outer(5)
    meet(1)
    qadd(2)
    outer(6)
    drain()

    def near_sum(s):
        for h in (0, 1):
            arrived(("p_up", s, h), pnear.at[s, 0, pl.ds(h * half, half)])
            arrived(("p_dn", s, h), pnear.at[s, 1, pl.ds(h * half, half)])

    near_sum(0)
    for h in (0, 1):
        at, piece = rows(1 - xh, y, h), pl.ds(h * half, half)
        total = acc[at, rcols[0]].astype(F32) + pnear[0, 0, piece].astype(F32) + pnear[0, 1, piece].astype(F32)
        acc[at, rcols[0]] = total.astype(BF16)
        send(("p_x", h), acc.at[at, rcols[0]], px.at[piece], over_x)
    qadd(3)
    for d in (0, 1):
        qfar_to(d)
    qnear_to(0, 1)
    qnear_to(1, 0)
    outer(7)
    for d, (name, b) in enumerate((("q_far_up", yp), ("q_far_dn", ym))):
        arrived((name, 0), qfar.at[d])
        add(rows(xh, b, d), 1, qfar.at[d])
        qnear_to(d, d)

    def finish(p, piece, total):
        gu[piece, rcols[p]] = (total * silu[piece, rcols[p]]).astype(BF16)
        gg[piece, rcols[p]] = (total * slope[piece, rcols[p]]).astype(BF16)

    near_sum(1)
    for h in (0, 1):
        piece = pl.ds(h * half, half)
        arrived(("p_x", h), px.at[piece])
        total = acc[rows(xh, y, h), rcols[0]].astype(F32) + px[piece].astype(F32)
        total = total + pnear[1, 0, piece].astype(F32) + pnear[1, 1, piece].astype(F32)
        finish(0, piece, total)
    for h in (0, 1):
        piece = pl.ds(h * half, half)
        arrived(("q_up", h), qnear.at[0, piece])
        arrived(("q_dn", h), qnear.at[1, piece])
        total = acc[rows(xh, y, h), rcols[1]].astype(F32)
        total = total + qnear[0, piece].astype(F32) + qnear[1, piece].astype(F32)
        finish(1, piece, total)
    stores.append(pltpu.make_async_copy(gg, gg_out, local.at[12]))
    stores.append(pltpu.make_async_copy(gu, gu_out, local.at[13]))
    stores[-1].start()
    stores[-2].start()
    for s in (0, 1):
        sent["p_far_up", s], sent["p_far_dn", s] = pfar.at[s, 0], pfar.at[s, 1]
        for h in (0, 1):
            sent["p_up", s, h] = sent["p_dn", s, h] = pnear.at[s, 0, pl.ds(h * half, half)]
    drain()
    for store in stores:
        store.wait()


def emit(gg_in, gu_in, gw_in, gg_out, gu_out, gw_out, sems):
    pieces = 8
    deep = gw_in.shape[0] // pieces
    copies = [pltpu.make_async_copy(gg_in, gg_out, sems.at[pieces]), pltpu.make_async_copy(gu_in, gu_out, sems.at[pieces + 1])]
    for i in range(pieces):
        at = pl.ds(i * deep, deep)
        copies.append(pltpu.make_async_copy(gw_in.at[at], gw_out.at[at], sems.at[i]))
    for copy in copies:
        copy.start()
    for copy in copies:
        copy.wait()


def on_device(grad_out, gate, up, w_down):
    own, units = gate.shape
    features = w_down.shape[0]
    tokens = own * NX * NY
    hsplit, split = 1024, 1024
    rest = units - split
    half = own // 2
    anywhere = pl.BlockSpec(memory_space=pl.ANY)
    results = pl.pallas_call(
        functools.partial(kernel, hsplit, split),
        out_shape=(
            jax.ShapeDtypeStruct((own, units), BF16),
            jax.ShapeDtypeStruct((own, units), BF16),
            jax.ShapeDtypeStruct((features, units), BF16),
        ),
        in_specs=[anywhere] * 4,
        out_specs=(anywhere,) * 3,
        scratch_shapes=[
            pltpu.VMEM((tokens, features), BF16),
            pltpu.VMEM((features, units), BF16),
            pltpu.VMEM((tokens, units), BF16),
            pltpu.VMEM((tokens, units), BF16),
            pltpu.VMEM((own, units), BF16),
            pltpu.VMEM((own, units), BF16),
            pltpu.VMEM((own, units), F32),
            pltpu.VMEM((own, units), F32),
            pltpu.VMEM((features, units), BF16),
            pltpu.VMEM((own, units), BF16),
            pltpu.VMEM((own, units), BF16),
            pltpu.VMEM((2, 2, half, split), BF16),
            pltpu.VMEM((2, 2, own, split), BF16),
            pltpu.VMEM((own, split), BF16),
            pltpu.VMEM((NY, own, rest), BF16),
            pltpu.VMEM((2, half, rest), BF16),
            pltpu.VMEM((2, own, rest), BF16),
            pltpu.SemaphoreType.DMA((14,)),
            pltpu.SemaphoreType.DMA((COPIES,)),
            pltpu.SemaphoreType.DMA((COPIES,)),
        ],
        compiler_params=pltpu.CompilerParams(
            collective_id=0, has_side_effects=True, vmem_limit_bytes=40 * 2**20
        ),
        cost_estimate=pl.CostEstimate(
            flops=4 * tokens * features * units, bytes_accessed=4 * features * units, transcendentals=own * units
        ),
    )(*[pltpu.with_memory_space_constraint(a, pltpu.HBM) for a in (grad_out, gate, up, w_down)])
    return pl.pallas_call(
        emit,
        out_shape=tuple(jax.ShapeDtypeStruct(r.shape, r.dtype) for r in results),
        in_specs=[pl.BlockSpec(memory_space=pl.ANY)] * 3,
        out_specs=(pl.BlockSpec(memory_space=pltpu.HBM),) * 3,
        scratch_shapes=[pltpu.SemaphoreType.DMA((10,))],
        compiler_params=pltpu.CompilerParams(vmem_limit_bytes=4 * 2**20),
    )(*[pltpu.with_memory_space_constraint(r, pltpu.VMEM) for r in results])


def solution(mesh):
    return jax.shard_map(
        on_device,
        mesh=mesh,
        in_specs=(P("col", "row"), P("row", "col"), P("row", "col"), P("row", "col")),
        out_specs=(P("row", "col"),) * 3,
        check_vma=False,
    )
```

time: 76.4 us -> 63.7 us (0.83)
  local copies, waits for them, and re-layouts: 9.89 us -> 0 us
  Pallas kernels: 65.6 us -> 63 us
    unnamed x3 -> x0, local copies, waits for them, and re-layouts: 9.89 us -> none
    pallas_call x1 -> x2, Pallas kernels: 65.6 us -> 63 us  [the longest x1 59.8 us: on_device(): pl.pallas_call(functools.partial(kernel, hsplit, split), out_shape=(jax.S...]
where the time goes in v2:
time: 63.7 us; the launch traced here: 63.6 us
  Pallas kernels  63 us (99%)
  between operations  0.64 us (1%)
    pallas_call x1, Pallas kernels, on_device(): pl.pallas_call(functools.partial(kernel, hsplit, split), out_shape=(jax.S...  59.8 us
    pallas_call x1, Pallas kernels, on_device(): pl.pallas_call(emit, out_shape=tuple((jax.ShapeDtypeStruct(r.shape, r.dty...  3.16 us

profile of v2, /device:TPU:0, one launch (start us, length us, event | category | flops | bytes accessed | tf_op | source)
XLA Modules:
  0.0 63.6 jit_solution(13600576133635821231)
XLA Ops:
  0.6 59.8 %shard_map.67 = (bf16[128,1664]{1,0:T(8,128)(2,1)S(1)}, bf16[128,1664]{1,0:T(8,128)(2,1)S(1)}, bf16[2048,1664]{1,0:T(8,128)(2,1)S(1)}) custom-call(bf16[64,2048]{1,0:T(8,128)(2,1)} %go_in.1, bf16[128,1664]{1,0:T(8,128)(2,1)} %gate_in.1, bf16[128,1664]{1,0:T(8,128)(2,1)} %up_in.1, bf16[2048,1664]{1,0:T(8,128)(2,1)} %w_in.1), custom_call_target="tpu_custom_call" | custom-call | flops 13958643712 | bytes 13631488 | tf_op jit(solution)/shard_map/pallas_call | solution.py:391
  60.4 3.2 %shard_map.68 = (bf16[128,1664]{1,0:T(8,128)(2,1)}, bf16[128,1664]{1,0:T(8,128)(2,1)}, bf16[2048,1664]{1,0:T(8,128)(2,1)}) custom-call(bf16[128,1664]{1,0:T(8,128)(2,1)S(1)} %get-tuple-element.6.gg_in, bf16[128,1664]{1,0:T(8,128)(2,1)S(1)} %get-tuple-element.7.gu_in, bf16[2048,1664]{1,0:T(8,128)(2,1)S(1)} %get-tuple-element.8.gw_in), custom_call_target="tpu_custom_call" | custom-call | tf_op jit(solution)/shard_map/pallas_call | solution.py:429

commit v3 on v2

--- a/solution.py
+++ b/solution.py
@@ -14,8 +14,8 @@
 
 
 def kernel(
-    hsplit, rsplit, go_in, gate_in, up_in, w_in, gg_out, gu_out, gw_out,
-    go, w, acc, hid, gate, up, silu, slope, gw, gg, gu,
+    hsplit, rsplit, go_in, gate_in, up_in, w_in, gg, gu, gw,
+    go, w, acc, hid, gate, up, silu, slope,
     pfar, pnear, px, qx, qfar, qnear, local, ssem, rsem,
 ):
     tokens, units = hid.shape
@@ -113,26 +113,25 @@
             slope[at, hcols[p]] = u * s * (1.0 + v * (1.0 - s))
             hid[to, hcols[p]] = (act * u).astype(BF16)
 
+    pl.semaphore_wait(barrier, len(peers))
+    pieces = [go_in.at[pl.ds(h * (part // 2), part // 2)] for h in (0, 1)]
+    for h in (0, 1):
+        gsend("g_next", xl, z, c, next_x, h, pieces[h])
+        gsend("g_up", xl, z, c, up_z, h, pieces[h])
+        gsend("g_dn", xl, z, c, dn_z, 1 - h, pieces[1 - h])
+    gsend("g_other", xl, z, c, other, src=go_in)
     loads[0].wait()
     loads[1].wait()
     loads[3].start()
     for p in (0, 1):
-        for h in (0, 1):
-            activate(p, h)
-    pl.semaphore_wait(barrier, len(peers))
-    pieces = [go_in.at[pl.ds(h * (part // 2), part // 2)] for h in (0, 1)]
-    for h in (0, 1):
-        gsend("g_next", xl, z, c, next_x, h, pieces[h])
-        gsend("g_up", xl, z, c, up_z, h, pieces[h])
-        gsend("g_dn", xl, z, c, dn_z, 1 - h, pieces[1 - h])
-        hsend("h_up", xh, y, 0, up_y, h)
-        hsend("h_dn", xh, y, 0, dn_y, 1 - h)
-        hsend("h_x", xh, y, 0, over_x, h)
-    for h in (0, 1):
-        hsend("h_up", xh, y, 1, up_y, h)
-        hsend("h_dn", xh, y, 1, dn_y, 1 - h)
-        hsend("h_x", xh, y, 1, over_x, h)
-    gsend("g_other", xl, z, c, other, src=go_in)
+        activate(p, 0)
+        hsend("h_up", xh, y, p, up_y, 0)
+        hsend("h_x", xh, y, p, over_x, 0)
+        activate(p, 1)
+        hsend("h_dn", xh, y, p, dn_y, 1)
+        hsend("h_x", xh, y, p, over_x, 1)
+        hsend("h_up", xh, y, p, up_y, 1)
+        hsend("h_dn", xh, y, p, dn_y, 0)
 
     def project(b):
         at = pl.ds(pl.multiple_of(b * group, group), group)
@@ -265,7 +264,6 @@
             add(rows(sides[s], b, d), 0, pfar.at[s, d])
             pnear_to(s, d, d)
 
-    stores = []
     deep = features // 8
 
     def outer(f):
@@ -273,9 +271,6 @@
         gw[at, :] = lax.dot_general(
             go[:, at], hid[...], (((0,), (0,)), ((), ())), preferred_element_type=F32
         ).astype(BF16)
-        store = pltpu.make_async_copy(gw.at[at], gw_out.at[at], local.at[4 + f])
-        store.start()
-        stores.append(store)
 
     def qadd(i):
         arrived(("q_x", i), qx.at[i])
@@ -302,23 +297,24 @@
     harrived("h_gdn", 1 - xh, yp, 0, 0)
     harrived("h_gup2", 1 - xh, yf, 0, 0)
     harrived("h_gdn2", 1 - xh, yf, 0, 1)
-    for f in range(4):
-        outer(f)
-    qadd(0)
-    outer(4)
-    qadd(1)
-    meet(0)
-    outer(5)
-    meet(1)
-    qadd(2)
-    outer(6)
-    drain()
-
     def near_sum(s):
         for h in (0, 1):
             arrived(("p_up", s, h), pnear.at[s, 0, pl.ds(h * half, half)])
             arrived(("p_dn", s, h), pnear.at[s, 1, pl.ds(h * half, half)])
 
+    outer(0)
+    outer(1)
+    outer(2)
+    outer(3)
+    meet(0)
+    qadd(0)
+    outer(4)
+    qadd(1)
+    meet(1)
+    outer(5)
+    qadd(2)
+    outer(6)
+    drain()
     near_sum(0)
     for h in (0, 1):
         at, piece = rows(1 - xh, y, h), pl.ds(h * half, half)
@@ -354,17 +350,11 @@
         total = acc[rows(xh, y, h), rcols[1]].astype(F32)
         total = total + qnear[0, piece].astype(F32) + qnear[1, piece].astype(F32)
         finish(1, piece, total)
-    stores.append(pltpu.make_async_copy(gg, gg_out, local.at[12]))
-    stores.append(pltpu.make_async_copy(gu, gu_out, local.at[13]))
-    stores[-1].start()
-    stores[-2].start()
     for s in (0, 1):
         sent["p_far_up", s], sent["p_far_dn", s] = pfar.at[s, 0], pfar.at[s, 1]
         for h in (0, 1):
             sent["p_up", s, h] = sent["p_dn", s, h] = pnear.at[s, 0, pl.ds(h * half, half)]
     drain()
-    for store in stores:
-        store.wait()
 
 
 def emit(gg_in, gu_in, gw_in, gg_out, gu_out, gw_out, sems):
@@ -396,7 +386,7 @@
             jax.ShapeDtypeStruct((features, units), BF16),
         ),
         in_specs=[anywhere] * 4,
-        out_specs=(anywhere,) * 3,
+        out_specs=(pl.BlockSpec(memory_space=pltpu.VMEM),) * 3,
         scratch_shapes=[
             pltpu.VMEM((tokens, features), BF16),
             pltpu.VMEM((features, units), BF16),
@@ -406,16 +396,13 @@
             pltpu.VMEM((own, units), BF16),
             pltpu.VMEM((own, units), F32),
             pltpu.VMEM((own, units), F32),
-            pltpu.VMEM((features, units), BF16),
-            pltpu.VMEM((own, units), BF16),
-            pltpu.VMEM((own, units), BF16),
             pltpu.VMEM((2, 2, half, split), BF16),
             pltpu.VMEM((2, 2, own, split), BF16),
             pltpu.VMEM((own, split), BF16),
             pltpu.VMEM((NY, own, rest), BF16),
             pltpu.VMEM((2, half, rest), BF16),
             pltpu.VMEM((2, own, rest), BF16),
-            pltpu.SemaphoreType.DMA((14,)),
+            pltpu.SemaphoreType.DMA((4,)),
             pltpu.SemaphoreType.DMA((COPIES,)),
             pltpu.SemaphoreType.DMA((COPIES,)),
         ],

time: 63.7 us -> 62.8 us (0.986)
  Pallas kernels: 63 us -> 61.8 us
    pallas_call x1, Pallas kernels: 59.8 us -> 58.6 us  [on_device(): pl.pallas_call(functools.partial(kernel, hsplit, split), out_shape=(jax.S...]
where the time goes in v3:
time: 62.8 us; the launch traced here: 62.4 us
  Pallas kernels  61.8 us (98%)
  between operations  0.64 us (1%)
    pallas_call x1, Pallas kernels, on_device(): pl.pallas_call(functools.partial(kernel, hsplit, split), out_shape=(jax.S...  58.6 us
    pallas_call x1, Pallas kernels, on_device(): pl.pallas_call(emit, out_shape=tuple((jax.ShapeDtypeStruct(r.shape, r.dty...  3.16 us

profile of v3, /device:TPU:0, one launch (start us, length us, event | category | flops | bytes accessed | tf_op | source)
XLA Modules:
  0.0 62.4 jit_solution(12433176819384358438)
XLA Ops:
  0.6 58.6 %shard_map.67 = (bf16[128,1664]{1,0:T(8,128)(2,1)S(1)}, bf16[128,1664]{1,0:T(8,128)(2,1)S(1)}, bf16[2048,1664]{1,0:T(8,128)(2,1)S(1)}) custom-call(bf16[64,2048]{1,0:T(8,128)(2,1)} %go_in.1, bf16[128,1664]{1,0:T(8,128)(2,1)} %gate_in.1, bf16[128,1664]{1,0:T(8,128)(2,1)} %up_in.1, bf16[2048,1664]{1,0:T(8,128)(2,1)} %w_in.1), custom_call_target="tpu_custom_call" | custom-call | flops 13958643712 | bytes 13631488 | tf_op jit(solution)/shard_map/pallas_call | solution.py:381
  59.3 3.2 %shard_map.68 = (bf16[128,1664]{1,0:T(8,128)(2,1)}, bf16[128,1664]{1,0:T(8,128)(2,1)}, bf16[2048,1664]{1,0:T(8,128)(2,1)}) custom-call(bf16[128,1664]{1,0:T(8,128)(2,1)S(1)} %get-tuple-element.6.gg_in, bf16[128,1664]{1,0:T(8,128)(2,1)S(1)} %get-tuple-element.7.gu_in, bf16[2048,1664]{1,0:T(8,128)(2,1)S(1)} %get-tuple-element.8.gw_in), custom_call_target="tpu_custom_call" | custom-call | tf_op jit(solution)/shard_map/pallas_call | solution.py:416

commit v4 on v3

--- a/solution.py
+++ b/solution.py
@@ -74,15 +74,17 @@
         pltpu.make_async_remote_copy(dst, dst, ssem.at[k], rsem.at[k], device_id=other, device_id_type=MESH).wait_recv()
 
     loads = [
-        pltpu.make_async_copy(gate_in, gate, local.at[0]),
-        pltpu.make_async_copy(up_in, up, local.at[1]),
-        pltpu.make_async_copy(go_in, go.at[panel(xl, z, c)], local.at[2]),
-        pltpu.make_async_copy(w_in, w, local.at[3]),
+        pltpu.make_async_copy(gate_in.at[:, hcols[0]], gate.at[:, hcols[0]], local.at[0]),
+        pltpu.make_async_copy(up_in.at[:, hcols[0]], up.at[:, hcols[0]], local.at[1]),
+        pltpu.make_async_copy(gate_in.at[:, hcols[1]], gate.at[:, hcols[1]], local.at[2]),
+        pltpu.make_async_copy(up_in.at[:, hcols[1]], up.at[:, hcols[1]], local.at[3]),
+        pltpu.make_async_copy(go_in, go.at[panel(xl, z, c)], local.at[4]),
+        pltpu.make_async_copy(w_in, w, local.at[5]),
     ]
     barrier = pltpu.get_barrier_semaphore()
     for peer in peers:
         pl.semaphore_signal(barrier, inc=1, device_id=peer, device_id_type=MESH)
-    for load in loads[:3]:
+    for load in loads[:5]:
         load.start()
 
     def gsend(name, a, b, d, device, h=None, src=None):
@@ -120,10 +122,11 @@
         gsend("g_up", xl, z, c, up_z, h, pieces[h])
         gsend("g_dn", xl, z, c, dn_z, 1 - h, pieces[1 - h])
     gsend("g_other", xl, z, c, other, src=go_in)
-    loads[0].wait()
-    loads[1].wait()
-    loads[3].start()
     for p in (0, 1):
+        loads[2 * p].wait()
+        loads[2 * p + 1].wait()
+        if p == 1:
+            loads[5].start()
         activate(p, 0)
         hsend("h_up", xh, y, p, up_y, 0)
         hsend("h_x", xh, y, p, over_x, 0)
@@ -213,8 +216,8 @@
     hsend("h_xm", xh, ym, 1, over_x, 1)
     harrived("h_dn", xh, yp, 1, 0)
     hsend("h_xp", xh, yp, 1, over_x, 0)
-    loads[2].wait()
-    loads[3].wait()
+    loads[4].wait()
+    loads[5].wait()
     garrived("g_other", xl, z, 1 - c)
     garrived("g_xother", 1 - xl, z, 1 - c, 0)
     garrived("g_xother", 1 - xl, z, 1 - c, 1)
@@ -315,9 +318,10 @@
     qadd(2)
     outer(6)
     drain()
-    near_sum(0)
     for h in (0, 1):
         at, piece = rows(1 - xh, y, h), pl.ds(h * half, half)
+        arrived(("p_up", 0, h), pnear.at[0, 0, piece])
+        arrived(("p_dn", 0, h), pnear.at[0, 1, piece])
         total = acc[at, rcols[0]].astype(F32) + pnear[0, 0, piece].astype(F32) + pnear[0, 1, piece].astype(F32)
         acc[at, rcols[0]] = total.astype(BF16)
         send(("p_x", h), acc.at[at, rcols[0]], px.at[piece], over_x)
@@ -402,7 +406,7 @@
             pltpu.VMEM((NY, own, rest), BF16),
             pltpu.VMEM((2, half, rest), BF16),
             pltpu.VMEM((2, own, rest), BF16),
-            pltpu.SemaphoreType.DMA((4,)),
+            pltpu.SemaphoreType.DMA((6,)),
             pltpu.SemaphoreType.DMA((COPIES,)),
             pltpu.SemaphoreType.DMA((COPIES,)),
         ],

time: 62.8 us -> 62.6 us (level)
  no operation moved by 1% of the time
where the time goes in v4:
time: 62.6 us; the launch traced here: 62.4 us
  Pallas kernels  61.8 us (99%)
  between operations  0.64 us (1%)
    pallas_call x1, Pallas kernels, on_device(): pl.pallas_call(functools.partial(kernel, hsplit, split), out_shape=(jax.S...  58.6 us
    pallas_call x1, Pallas kernels, on_device(): pl.pallas_call(emit, out_shape=tuple((jax.ShapeDtypeStruct(r.shape, r.dty...  3.16 us

profile of v4, /device:TPU:0, one launch (start us, length us, event | category | flops | bytes accessed | tf_op | source)
XLA Modules:
  0.0 62.4 jit_solution(6765578035307111736)
XLA Ops:
  0.6 58.6 %shard_map.67 = (bf16[128,1664]{1,0:T(8,128)(2,1)S(1)}, bf16[128,1664]{1,0:T(8,128)(2,1)S(1)}, bf16[2048,1664]{1,0:T(8,128)(2,1)S(1)}) custom-call(bf16[64,2048]{1,0:T(8,128)(2,1)} %go_in.1, bf16[128,1664]{1,0:T(8,128)(2,1)} %gate_in.1, bf16[128,1664]{1,0:T(8,128)(2,1)} %up_in.1, bf16[2048,1664]{1,0:T(8,128)(2,1)} %w_in.1), custom_call_target="tpu_custom_call" | custom-call | flops 13958643712 | bytes 13631488 | tf_op jit(solution)/shard_map/pallas_call | solution.py:385
  59.3 3.2 %shard_map.68 = (bf16[128,1664]{1,0:T(8,128)(2,1)}, bf16[128,1664]{1,0:T(8,128)(2,1)}, bf16[2048,1664]{1,0:T(8,128)(2,1)}) custom-call(bf16[128,1664]{1,0:T(8,128)(2,1)S(1)} %get-tuple-element.6.gg_in, bf16[128,1664]{1,0:T(8,128)(2,1)S(1)} %get-tuple-element.7.gu_in, bf16[2048,1664]{1,0:T(8,128)(2,1)S(1)} %get-tuple-element.8.gw_in), custom_call_target="tpu_custom_call" | custom-call | tf_op jit(solution)/shard_map/pallas_call | solution.py:420

commit v5 on v4

--- a/solution.py
+++ b/solution.py
@@ -347,6 +347,11 @@
         total = acc[rows(xh, y, h), rcols[0]].astype(F32) + px[piece].astype(F32)
         total = total + pnear[1, 0, piece].astype(F32) + pnear[1, 1, piece].astype(F32)
         finish(0, piece, total)
+    for s in (0, 1):
+        sent["p_far_up", s], sent["p_far_dn", s] = pfar.at[s, 0], pfar.at[s, 1]
+        for h in (0, 1):
+            sent["p_up", s, h] = sent["p_dn", s, h] = pnear.at[s, 0, pl.ds(h * half, half)]
+    drain()
     for h in (0, 1):
         piece = pl.ds(h * half, half)
         arrived(("q_up", h), qnear.at[0, piece])
@@ -354,11 +359,6 @@
         total = acc[rows(xh, y, h), rcols[1]].astype(F32)
         total = total + qnear[0, piece].astype(F32) + qnear[1, piece].astype(F32)
         finish(1, piece, total)
-    for s in (0, 1):
-        sent["p_far_up", s], sent["p_far_dn", s] = pfar.at[s, 0], pfar.at[s, 1]
-        for h in (0, 1):
-            sent["p_up", s, h] = sent["p_dn", s, h] = pnear.at[s, 0, pl.ds(h * half, half)]
-    drain()
 
 
 def emit(gg_in, gu_in, gw_in, gg_out, gu_out, gw_out, sems):

time: 62.6 us -> 62.6 us (level)
  no operation moved by 1% of the time
where the time goes in v5:
time: 62.6 us; the launch traced here: 62.4 us
  Pallas kernels  61.8 us (99%)
  between operations  0.64 us (1%)
    pallas_call x1, Pallas kernels, on_device(): pl.pallas_call(functools.partial(kernel, hsplit, split), out_shape=(jax.S...  58.6 us
    pallas_call x1, Pallas kernels, on_device(): pl.pallas_call(emit, out_shape=tuple((jax.ShapeDtypeStruct(r.shape, r.dty...  3.16 us

profile of v5, /device:TPU:0, one launch (start us, length us, event | category | flops | bytes accessed | tf_op | source)
XLA Modules:
  0.0 62.4 jit_solution(4473176648284795519)
XLA Ops:
  0.6 58.6 %shard_map.67 = (bf16[128,1664]{1,0:T(8,128)(2,1)S(1)}, bf16[128,1664]{1,0:T(8,128)(2,1)S(1)}, bf16[2048,1664]{1,0:T(8,128)(2,1)S(1)}) custom-call(bf16[64,2048]{1,0:T(8,128)(2,1)} %go_in.1, bf16[128,1664]{1,0:T(8,128)(2,1)} %gate_in.1, bf16[128,1664]{1,0:T(8,128)(2,1)} %up_in.1, bf16[2048,1664]{1,0:T(8,128)(2,1)} %w_in.1), custom_call_target="tpu_custom_call" | custom-call | flops 13958643712 | bytes 13631488 | tf_op jit(solution)/shard_map/pallas_call | solution.py:385
  59.2 3.2 %shard_map.68 = (bf16[128,1664]{1,0:T(8,128)(2,1)}, bf16[128,1664]{1,0:T(8,128)(2,1)}, bf16[2048,1664]{1,0:T(8,128)(2,1)}) custom-call(bf16[128,1664]{1,0:T(8,128)(2,1)S(1)} %get-tuple-element.6.gg_in, bf16[128,1664]{1,0:T(8,128)(2,1)S(1)} %get-tuple-element.7.gu_in, bf16[2048,1664]{1,0:T(8,128)(2,1)S(1)} %get-tuple-element.8.gw_in), custom_call_target="tpu_custom_call" | custom-call | tf_op jit(solution)/shard_map/pallas_call | solution.py:420
